TPU v7x, 32 devices: a whole 2x2x4 slice. The times are simulated.
32 devices in a mesh: groups: 2 (over y), blk: 16 (over z, x, core).
Axes of the slice: x: 2, y: 2, z: 4, core: 2. Of those that a mesh axis runs over, the one named last changes fastest.
Arguments:
- queries: bfloat16 [128, 4096], P(('groups', 'blk')), parts along dimension 0, may hold values from -150 to 150
- k_cache: bfloat16 [32768, 512], P(('groups', 'blk')), parts along dimension 0, may hold values from -6 to 6
- v_cache: bfloat16 [32768, 512], P(('groups', 'blk')), parts along dimension 0, may hold values from -6 to 6
- w_out: bfloat16 [4096, 2048], P('blk'), may hold values from -0.09375 to 0.09375
- residual: bfloat16 [128, 2048], P(('groups', 'blk')), parts along dimension 0, may hold values from -6 to 6
- norm_gain: float32 [2048], replicated, may hold values from 0.1 to 1.9
- expert_ids: int32 [128, 8], P('groups'), parts along dimension 0, may hold values from 0 to 15, all different within a row; in each aligned block of 64 rows (0 to 63, 64 to 127, ...) at most 64 rows name the same one
- gate_fixed: int32 [128, 8], P('groups'), parts along dimension 0, may hold values from 1 to 65535
- w_gate: bfloat16 [16, 2048, 768], P('blk'), may hold values from -0.125 to 0.125
- w_up: bfloat16 [16, 2048, 768], P('blk'), may hold values from -0.125 to 0.125
- w_down: bfloat16 [16, 768, 2048], P('blk'), may hold values from -0.21875 to 0.21875
Outputs:
- hidden: bfloat16 [128, 2048], P(('groups', 'blk')), parts along dimension 0
- moe_out: bfloat16 [128, 2048], P(('groups', 'blk')), parts along dimension 0
There are 2 independent parts, one for each index of `groups`. A program takes and returns all parts, laid end to end along the dimension named above; an argument that names none is the same for every part. Nothing has to cross between parts.
Inputs may be any that keep to these rules, and one draw needn't show every extreme that they name: `expert_ids`: each row names 8 different experts; no expert is named by more than 64 rows of a part, a bound that some block reaches.
All inputs are finite; a program needn't handle non-finite values.
Results may differ from a plain program's by a relative error of at most 0.0075.
Values may be sent and summed in bfloat16 or wider, within the bound.
A program may use at most 128 MiB of HBM per device.

v0:
```python
import jax
import jax.numpy as jnp
from jax import lax
from jax.sharding import PartitionSpec as P

HEADS = 32
KV_HEADS = 4
HEAD_DIM = 128
GROUP = 8
CAPACITY = 64


def local_attend(query_rows, k_cache, v_cache):
    row_count = query_rows.shape[0]
    span = k_cache.shape[0]
    query_four = query_rows.reshape(row_count, KV_HEADS, GROUP, HEAD_DIM)
    key_three = k_cache.reshape(span, KV_HEADS, HEAD_DIM)
    value_three = v_cache.reshape(span, KV_HEADS, HEAD_DIM)
    scores = jnp.einsum(
        "rhgd,chd->rhgc", query_four, key_three, preferred_element_type=jnp.float32
    ) / jnp.sqrt(jnp.float32(HEAD_DIM))
    block_max = jnp.max(scores, axis=-1)
    probs = jnp.exp(scores - block_max[..., None])
    block_sum = jnp.sum(probs, axis=-1)
    block_out = jnp.einsum(
        "rhgc,chd->rhgd",
        probs.astype(jnp.bfloat16),
        value_three,
        preferred_element_type=jnp.float32,
    )
    return (
        block_out.reshape(row_count, HEADS * HEAD_DIM),
        block_max.reshape(row_count, HEADS),
        block_sum.reshape(row_count, HEADS),
    )


def shards(
    queries,
    k_cache,
    v_cache,
    w_out,
    residual,
    norm_gain,
    expert_ids,
    gate_fixed,
    w_gate,
    w_up,
    w_down,
):
    row_count = queries.shape[0]
    width_q = HEADS * HEAD_DIM
    devices = lax.axis_size("blk")
    every_query = lax.all_gather(queries, "blk", axis=0, tiled=True)
    total_rows = every_query.shape[0]
    block_rows = 128 if total_rows % 128 == 0 else total_rows
    stacked = every_query.reshape(total_rows // block_rows, block_rows, width_q)
    part_out, part_max, part_sum = lax.map(
        lambda piece: local_attend(piece, k_cache, v_cache), stacked
    )
    part_out = part_out.reshape(total_rows, width_q)
    part_max = part_max.reshape(total_rows, HEADS)
    part_sum = part_sum.reshape(total_rows, HEADS)
    got_out, got_max, got_sum = (
        lax.all_to_all(part_out, "blk", split_axis=0, concat_axis=0, tiled=True),
        lax.all_to_all(part_max, "blk", split_axis=0, concat_axis=0, tiled=True),
        lax.all_to_all(part_sum, "blk", split_axis=0, concat_axis=0, tiled=True),
    )
    got_out = got_out.reshape(devices, row_count, HEADS, HEAD_DIM)
    got_max = got_max.reshape(devices, row_count, HEADS)
    got_sum = got_sum.reshape(devices, row_count, HEADS)
    top = jnp.max(got_max, axis=0)
    factor = jnp.exp(got_max - top[None])
    sum_acc = jnp.sum(got_sum * factor, axis=0)
    out_acc = jnp.sum(got_out * factor[..., None], axis=0).reshape(row_count, width_q)
    attended = (
        (out_acc.reshape(row_count, HEADS, HEAD_DIM) / sum_acc[..., None])
        .reshape(row_count, width_q)
        .astype(jnp.bfloat16)
    )
    columns = lax.all_to_all(attended, "blk", split_axis=1, concat_axis=0, tiled=True)
    piece = columns
    proj = lax.psum_scatter(
        jnp.dot(piece, w_out, preferred_element_type=jnp.float32),
        "blk",
        scatter_dimension=0,
        tiled=True,
    )
    stream = residual.astype(jnp.float32) + proj
    hidden = stream.astype(jnp.bfloat16)
    normed = (
        stream * lax.rsqrt(jnp.mean(stream * stream, axis=-1, keepdims=True) + 1e-06) * norm_gain
    ).astype(jnp.bfloat16)
    every_row = lax.all_gather(normed, "blk", axis=0, tiled=True)
    expert = lax.axis_index("blk")
    named = expert_ids == expert
    taken = jnp.any(named, axis=1)
    row_weight = jnp.sum(jnp.where(named, gate_fixed.astype(jnp.float32) / 65536.0, 0.0), axis=1)
    slot_of = jnp.cumsum(taken.astype(jnp.int32)) - 1
    slot_ids = jnp.arange(CAPACITY, dtype=jnp.int32)
    select = jnp.logical_and(slot_of[None, :] == slot_ids[:, None], taken[None, :])
    picked = jnp.dot(
        select.astype(jnp.bfloat16), every_row, preferred_element_type=jnp.float32
    ).astype(jnp.bfloat16)
    slot_weight = jnp.dot(select.astype(jnp.float32), row_weight, precision=lax.Precision.HIGHEST)
    gate_part = jnp.dot(picked, w_gate[0], preferred_element_type=jnp.float32)
    up_part = jnp.dot(picked, w_up[0], preferred_element_type=jnp.float32)
    inner = (jax.nn.silu(gate_part) * up_part).astype(jnp.bfloat16)
    result = jnp.dot(inner, w_down[0], preferred_element_type=jnp.float32) * slot_weight[:, None]
    select_back = select.astype(jnp.float32).T
    piece = select_back
    moe_total = lax.psum_scatter(
        jnp.dot(piece, result, precision=lax.Precision.HIGHEST),
        "blk",
        scatter_dimension=0,
        tiled=True,
    )
    return (hidden, moe_total.astype(jnp.bfloat16))


def solution(mesh):
    return jax.shard_map(
        shards,
        mesh=mesh,
        in_specs=(
            P(("groups", "blk"), None),
            P(("groups", "blk"), None),
            P(("groups", "blk"), None),
            P("blk", None),
            P(("groups", "blk"), None),
            P(),
            P("groups", None),
            P("groups", None),
            P("blk", None, None),
            P("blk", None, None),
            P("blk", None, None),
        ),
        out_specs=(P(("groups", "blk"), None), P(("groups", "blk"), None)),
        check_vma=False,
    )
```

profile of v0, /device:TPU:0, one launch (start us, length us, event | category | flops | bytes accessed | tf_op | source)
XLA Modules:
  0.0 310.2 jit_solution(18031536088739600223)
XLA Ops:
  7.2 2.3 reshape.113
  9.5 26.3 %all-gather = bf16[16,4,4096]{2,1,0:T(4,128)(2,1)} all-gather(bf16[1,4,4096]{2,1,0:T(4,128)(2,1)} %bitcast.64), channel_id=1, replica_groups=mesh['groups'=2,'blk'=16] {'blk'}, dimensions={0}, use_global_device_ids=true | all-gather | bytes 557056 | tf_op jit(solution)/shard_map/all_gather | solution.py:54
  35.8 2.4 reshape.112
  38.2 2.7 bitcast_reduce_fusion
  40.9 3.2 %copy-done.1 = f32[4,64,8,1024]{3,2,1,0:T(8,128)} copy-done((f32[4,64,8,1024]{3,2,1,0:T(8,128)}, f32[4,64,8,1024]{3,2,1,0:T(8,128)S(1)}, u32[]{:S(2)}) %copy-start.1) | copy-done | bytes 8388632
  44.1 1.9 fusion.1
  46.0 0.1 copy.34
  46.1 0.1 all_to_all.34
  46.2 0.7 reshape.128
  46.9 3.5 %all-to-all-start.2 = ((f32[16,1,128]{2,1,0:T(1,128)}), f32[16,1,128]{2,1,0:T(1,128)S(1)}, u32[]{:S(2)}, u32[]{:S(2)}) async-start(f32[16,1,128]{2,1,0:T(1,128)} %reshape.128), calls=%async_computation.2 | async-start | bytes 16384 | tf_op jit(solution)/shard_map/all_to_all | solution.py:67
  50.4 0.1 copy.33
  50.5 0.1 all_to_all.32
  50.6 0.7 reshape.130
  51.3 2.2 reshape.114
  53.5 3.1 %all-to-all-done.2 = f32[16,1,128]{2,1,0:T(1,128)S(1)} async-done(((f32[16,1,128]{2,1,0:T(1,128)}), f32[16,1,128]{2,1,0:T(1,128)S(1)}, u32[]{:S(2)}, u32[]{:S(2)}) %all-to-all-start.2) | async-done | bytes 8224 | tf_op jit(solution)/shard_map/all_to_all | solution.py:67
  56.7 3.5 %all-to-all-start.1 = ((f32[16,1,128]{2,1,0:T(1,128)}), f32[16,1,128]{2,1,0:T(1,128)S(1)}, u32[]{:S(2)}, u32[]{:S(2)}) async-start(f32[16,1,128]{2,1,0:T(1,128)} %reshape.130), calls=%async_computation.1 | async-start | bytes 16384 | tf_op jit(solution)/shard_map/all_to_all | solution.py:66
  60.2 4.8 %fusion.16 = f32[64,4,8,128]{3,2,0,1:T(8,128)S(1)} fusion(f32[4,64,8,1024]{3,2,1,0:T(8,128)} %copy-done.1, f32[64,4,8]{2,0,1:T(8,128)S(1)} %get-tuple-element.29, bf16[1024,4,128,1]{2,1,0,3:T(4,128)(2,1)} %bitcast.61), kind=kOutput, calls=%fused_computation.16 | convolution fusion | flops 543162368 | bytes 10493952 | tf_op jit(solution)/shard_map/while/body/eval_jaxpr/rhgc,chd->rhgd/dot_general | solution.py:25
  65.0 1.2 copy.32
  66.2 2.6 all_to_all.30
  68.8 6.0 %all-to-all-start = ((f32[16,4,4096]{2,1,0:T(4,128)}), f32[16,4,4096]{2,1,0:T(4,128)}, u32[]{:S(2)}, u32[]{:S(2)}) async-start(f32[16,4,4096]{2,1,0:T(4,128)} %all_to_all.30), calls=%async_computation | async-start | bytes 2097152 | tf_op jit(solution)/shard_map/all_to_all | solution.py:65
  74.8 0.5 broadcast.64
  75.3 0.7 reduce.4
  76.1 0.7 reduce.5
  76.7 0.1 reshape.131
  77.0 1.3 mul.48
  78.3 2.6 mul.49
  80.9 16.9 %all-to-all-done = f32[16,4,4096]{2,1,0:T(4,128)} async-done(((f32[16,4,4096]{2,1,0:T(4,128)}), f32[16,4,4096]{2,1,0:T(4,128)}, u32[]{:S(2)}, u32[]{:S(2)}) %all-to-all-start) | async-done | bytes 1048608 | tf_op jit(solution)/shard_map/all_to_all | solution.py:65
  97.8 1.9 multiply_reduce_fusion
  99.7 0.6 copy.35
  100.3 6.9 %all-to-all-start.3 = ((bf16[4,16,256]{2,0,1:T(4,128)(2,1)}), bf16[4,16,256]{2,0,1:T(4,128)(2,1)S(1)}, u32[]{:S(2)}, u32[]{:S(2)}) async-start(bf16[4,16,256]{2,0,1:T(4,128)(2,1)} %copy.35), calls=%async_computation.3 | async-start | bytes 65536 | tf_op jit(solution)/shard_map/all_to_all | solution.py:81
  107.3 6.5 %all-to-all-done.3 = bf16[4,16,256]{2,0,1:T(4,128)(2,1)S(1)} async-done(((bf16[4,16,256]{2,0,1:T(4,128)(2,1)}), bf16[4,16,256]{2,0,1:T(4,128)(2,1)S(1)}, u32[]{:S(2)}, u32[]{:S(2)}) %all-to-all-start.3) | async-done | bytes 32800 | tf_op jit(solution)/shard_map/all_to_all | solution.py:81
  113.8 2.3 fusion.54
  116.2 0.1 copy.36
  116.3 0.6 dynamic-slice.1
  117.5 0.1 reduce-window.8
  117.6 0.1 add_reduce_fusion
  117.7 0.1 convolution_bitcast_fusion
  117.8 85.7 %all-reduce.5.cloned.1.call-done = f32[64,2048]{1,0:T(8,128)} async-done(((f32[64,2048]{1,0:T(8,128)}), f32[64,2048]{1,0:T(8,128)}) %all-reduce.5.cloned.1.call-update) | async-done | bytes 524304
  203.6 1.0 multiply_reduce_fusion.1
  204.6 1.5 fusion.43
  206.1 21.5 %all-gather.1 = bf16[16,4,2048]{2,1,0:T(4,128)(2,1)S(1)} all-gather(bf16[1,4,2048]{2,1,0:T(4,128)(2,1)S(1)} %get-tuple-element.20), channel_id=1, replica_groups=mesh['groups'=2,'blk'=16] {'blk'}, dimensions={0}, use_global_device_ids=true | all-gather | bytes 278528 | tf_op jit(solution)/shard_map/all_gather | solution.py:94
  227.6 0.8 reshape.119
  228.3 1.2 convolution_convert_fusion
  229.5 3.2 %fusion.11 = f32[64,768]{1,0:T(8,128)} fusion(bf16[64,2048]{1,0:T(8,128)(2,1)S(1)} %convolution_convert_fusion, bf16[1,2048,768]{2,1,0:T(8,128)(2,1)} %param.19), kind=kOutput, calls=%fused_computation.12 | convolution fusion | flops 201326592 | bytes 3604480 | tf_op jit(solution)/shard_map/dot_general | solution.py:106
  232.7 4.0 %fusion.13 = f32[64,2048]{1,0:T(8,128)} fusion(bf16[1,768,2048]{2,1,0:T(8,128)(2,1)S(1)} %copy-done, bf16[64,2048]{1,0:T(8,128)(2,1)S(1)} %convolution_convert_fusion, bf16[1,2048,768]{2,1,0:T(8,128)(2,1)} %param.20, f32[64]{0:T(128)S(1)} %convolution_bitcast_fusion, f32[64,768]{1,0:T(8,128)} %fusion.11), kind=kOutput, calls=%fused_computation.14 | convolution fusion | flops 403079168 | bytes 7274752 | tf_op jit(solution)/shard_map/dot_general | solution.py:109
  236.7 2.3 fusion.39
  239.0 63.7 %all-reduce.6 = bf16[64,2048]{1,0:T(8,128)(2,1)S(1)} all-reduce(f32[64,2048]{1,0:T(8,128)} %fusion.39), channel_id=3, replica_groups=mesh['groups'=2,'blk'=16] {'blk'}, use_global_device_ids=true, to_apply=%region_10.11.clone | all-reduce | flops 131072 | bytes 786432
  302.7 0.6 dynamic-slice_convert_fusion
  (27 shorter events, 0.5 us)
Async XLA Ops:
  7.2 225.6 %copy-start = (bf16[1,768,2048]{2,1,0:T(8,128)(2,1)S(1)}, bf16[1,768,2048]{2,1,0:T(8,128)(2,1)}, u32[]{:S(2)}) copy-start(bf16[1,768,2048]{2,1,0:T(8,128)(2,1)} %param.21) | copy-start | bytes 9437188
  40.9 3.2 %copy-start.1 = (f32[4,64,8,1024]{3,2,1,0:T(8,128)}, f32[4,64,8,1024]{3,2,1,0:T(8,128)S(1)}, u32[]{:S(2)}) copy-start(f32[4,64,8,1024]{3,2,1,0:T(8,128)S(1)} %get-tuple-element.30) | copy-start | bytes 25165828
  46.9 9.8 %all-to-all-start.2 = ((f32[16,1,128]{2,1,0:T(1,128)}), f32[16,1,128]{2,1,0:T(1,128)S(1)}, u32[]{:S(2)}, u32[]{:S(2)}) async-start(f32[16,1,128]{2,1,0:T(1,128)} %reshape.128), calls=%async_computation.2 | async-start | bytes 16384 | tf_op jit(solution)/shard_map/all_to_all | solution.py:67
  56.7 12.1 %all-to-all-start.1 = ((f32[16,1,128]{2,1,0:T(1,128)}), f32[16,1,128]{2,1,0:T(1,128)S(1)}, u32[]{:S(2)}, u32[]{:S(2)}) async-start(f32[16,1,128]{2,1,0:T(1,128)} %reshape.130), calls=%async_computation.1 | async-start | bytes 16384 | tf_op jit(solution)/shard_map/all_to_all | solution.py:66
  65.0 42.3 %copy-start.4 = (s32[64,8]{0,1:T(8,128)S(1)}, s32[64,8]{0,1:T(8,128)}, u32[]{:S(2)}) copy-start(s32[64,8]{0,1:T(8,128)} %param.18) | copy-start | bytes 6148
  65.0 42.2 %copy-start.5 = (s32[64,8]{0,1:T(8,128)S(1)}, s32[64,8]{0,1:T(8,128)}, u32[]{:S(2)}) copy-start(s32[64,8]{0,1:T(8,128)} %param.17) | copy-start | bytes 6148
  65.0 51.3 %copy-start.6 = (u32[32]{0:T(128)S(1)}, u32[32]{0:T(128)}, u32[]{:S(2)}) copy-start(u32[32]{0:T(128)} %constant.57) | copy-start | bytes 388
  65.0 138.6 %copy-start.2 = (bf16[4,2048]{1,0:T(4,128)(2,1)S(1)}, bf16[4,2048]{1,0:T(4,128)(2,1)}, u32[]{:S(2)}) copy-start(bf16[4,2048]{1,0:T(4,128)(2,1)} %param.15) | copy-start | bytes 49156
  65.0 139.6 %copy-start.3 = (f32[2048]{0:T(1024)S(1)}, f32[2048]{0:T(1024)}, u32[]{:S(2)}) copy-start(f32[2048]{0:T(1024)} %param.16) | copy-start | bytes 24580
  68.8 29.0 %all-to-all-start = ((f32[16,4,4096]{2,1,0:T(4,128)}), f32[16,4,4096]{2,1,0:T(4,128)}, u32[]{:S(2)}, u32[]{:S(2)}) async-start(f32[16,4,4096]{2,1,0:T(4,128)} %all_to_all.30), calls=%async_computation | async-start | bytes 2097152 | tf_op jit(solution)/shard_map/all_to_all | solution.py:65
  100.3 13.5 %all-to-all-start.3 = ((bf16[4,16,256]{2,0,1:T(4,128)(2,1)}), bf16[4,16,256]{2,0,1:T(4,128)(2,1)S(1)}, u32[]{:S(2)}, u32[]{:S(2)}) async-start(bf16[4,16,256]{2,0,1:T(4,128)(2,1)} %copy.35), calls=%async_computation.3 | async-start | bytes 65536 | tf_op jit(solution)/shard_map/all_to_all | solution.py:81
  107.2 96.4 %all-reduce.5.cloned.1.call-start = ((), (), s32[]{:S(2)}) async-start(), calls=%async_computation.4 | async-start | bytes 1048576
Sparse Core Ops, SparseCore 0:
  116.3 87.2 all-reduce.4
where the time goes:
time: 311 us; the launch traced here: 310 us
  waiting for transfers between devices  112 us (36%)
  blocking collectives  111 us (36%)
  local copies, waits for them, and re-layouts  23.1 us (7%)
  matrix products  20.6 us (7%)
  starting transfers between devices  19.9 us (6%)
  between operations  14.9 us (5%)
  other arithmetic  7.85 us (3%)
    unnamed x2, waiting for transfers between devices  85.8 us
    unnamed x1, blocking collectives  63.7 us
    all_gather x1, blocking collectives, shards(): every_query = lax.all_gather(queries, 'blk', axis=0, tiled=True)  26.3 us
    all_gather x1, blocking collectives, shards(): every_row = lax.all_gather(normed, 'blk', axis=0, tiled=True)  21.5 us
    all_to_all x1, waiting for transfers between devices, shards(): lax.all_to_all(part_out, 'blk', split_axis=0, concat_axis=0, tiled=True)  16.9 us
    all_to_all x1, starting transfers between devices, shards(): lax.all_to_all(attended, 'blk', split_axis=1, concat_axis=0, tiled=True)  6.86 us
    all_to_all x1, waiting for transfers between devices, shards(): lax.all_to_all(attended, 'blk', split_axis=1, concat_axis=0, tiled=True)  6.52 us
  transfers between devices with their start and end apart: 5, of which 4 were waited for; matrix products, arithmetic and copies ran while one was open for 5% of the time, Pallas kernels for 0%

commit v1 on v0

--- a/solution.py
+++ b/solution.py
@@ -1,6 +1,11 @@
+import functools
+import math
+
 import jax
 import jax.numpy as jnp
 from jax import lax
+from jax.experimental import pallas as pl
+from jax.experimental.pallas import tpu as pltpu
 from jax.sharding import PartitionSpec as P
 
 HEADS = 32
@@ -96,7 +101,9 @@
     named = expert_ids == expert
     taken = jnp.any(named, axis=1)
     row_weight = jnp.sum(jnp.where(named, gate_fixed.astype(jnp.float32) / 65536.0, 0.0), axis=1)
-    slot_of = jnp.cumsum(taken.astype(jnp.int32)) - 1
+    order = jnp.arange(taken.shape[0], dtype=jnp.int32)
+    upto = jnp.logical_and(order[None, :] <= order[:, None], taken[None, :])
+    slot_of = jnp.sum(upto.astype(jnp.int32), axis=1) - 1
     slot_ids = jnp.arange(CAPACITY, dtype=jnp.int32)
     select = jnp.logical_and(slot_of[None, :] == slot_ids[:, None], taken[None, :])
     picked = jnp.dot(
@@ -118,9 +125,272 @@
     return (hidden, moe_total.astype(jnp.bfloat16))
 
 
+MESH = pl.DeviceIdType.MESH
+TILE = 16
+F32, BF16 = jnp.float32, jnp.bfloat16
+
+
+def fits_fused(n, queries, k_cache, v_cache, w_out, residual, gain, ids, gates, w_gate, w_up, w_down):
+    rows, width = queries.shape
+    heads = width // HEAD_DIM
+    return (
+        heads % n == 0
+        and w_out.shape[0] % HEAD_DIM == 0
+        and GROUP % (heads // n) == 0
+        and (heads // n) * n * rows == HEAD_DIM
+        and w_gate.shape[0] == 1
+        and TILE % rows == 0
+        and n * TILE == 256
+        and residual.shape[1] % (TILE // rows * 128) == 0
+    )
+
+
+def select(out_rows, in_rows, source):
+    o = lax.broadcasted_iota(jnp.int32, (out_rows, in_rows), 0)
+    i = lax.broadcasted_iota(jnp.int32, (out_rows, in_rows), 1)
+    return jnp.where(i == source(o), 1.0, 0.0).astype(BF16)
+
+
+def dot(a, b, ca=1, cb=0):
+    return lax.dot_general(a, b, (((ca,), (cb,)), ((), ())), preferred_element_type=F32)
+
+
+def fused_kernel(
+    n, q_ref, res_ref, gain_ref, ids_ref, gates_ref, k_hbm, v_hbm, wo_hbm, wg_hbm, wu_hbm, wd_hbm,
+    hid_ref, moe_ref,
+    k_buf, v_buf, wo_buf, wg_buf, wu_buf, wd_buf, q_tmp, t_tmp, s_tmp,
+    q_all, o_send, o_got, s_send, s_got, p_send, p_got, n_all, y_send, y_got,
+    load_sem, q_ss, q_rs, o_ss, o_rs, s_ss, s_rs, p_ss, p_rs, n_ss, n_rs, y_ss, y_rs,
+):
+    me = lax.axis_index("blk")
+    rows, width = q_ref.shape
+    model = res_ref.shape[1]
+    heads = width // HEAD_DIM
+    kv = heads // GROUP
+    own_heads = heads // n
+    per_kv = GROUP // own_heads
+    total = n * rows
+    parts = TILE // rows
+    cols = model // parts
+    div, rem = lax.div, lax.rem
+    scale = math.log2(math.e) / math.sqrt(HEAD_DIM)
+
+    loads = [
+        pltpu.make_async_copy(s, d, load_sem.at[i])
+        for i, (s, d) in enumerate(
+            ((k_hbm, k_buf), (v_hbm, v_buf), (wo_hbm, wo_buf), (wg_hbm.at[0], wg_buf), (wu_hbm.at[0], wu_buf), (wd_hbm.at[0], wd_buf))
+        )
+    ]
+    for load in loads:
+        load.start()
+
+    barrier = pltpu.get_barrier_semaphore()
+
+    def greet(k, _):
+        pl.semaphore_signal(barrier, inc=1, device_id={"blk": rem(me + k, n)}, device_id_type=MESH)
+        return 0
+
+    lax.fori_loop(1, n, greet, 0)
+
+    def remote(src, dst, ss, rs, k):
+        return pltpu.make_async_remote_copy(
+            src_ref=src, dst_ref=dst, send_sem=ss.at[k], recv_sem=rs.at[k],
+            device_id={"blk": rem(me + k, n)}, device_id_type=MESH,
+        )
+
+    def spread(make):
+        def step(k, _):
+            make(k).start()
+            return 0
+
+        lax.fori_loop(1, n, step, 0)
+
+    def arrive(make):
+        def step(k, _):
+            make(k).wait_recv()
+            return 0
+
+        lax.fori_loop(1, n, step, 0)
+
+    def left(make):
+        def step(k, _):
+            make(k).wait_send()
+            return 0
+
+        lax.fori_loop(1, n, step, 0)
+
+    for h in range(heads):
+        q_tmp[h * rows : (h + 1) * rows, :] = q_ref[:, h * HEAD_DIM : (h + 1) * HEAD_DIM].astype(F32)
+    q_all[me] = q_tmp[...].astype(BF16)
+    pl.semaphore_wait(barrier, n - 1)
+    send_q = lambda k: remote(q_all.at[me], q_all.at[me], q_ss, q_rs, k)
+    spread(send_q)
+
+    for c in range(parts):
+        t_tmp[c * rows : (c + 1) * rows, :] = res_ref[:, c * cols : (c + 1) * cols].astype(F32)
+    spread_rows = lambda o: div(o, TILE) * rows + rem(o, rows)
+    repeat = select(n * TILE, total, spread_rows)
+    part_of = div(rem(lax.broadcasted_iota(jnp.int32, (n * TILE, 1), 0), TILE), rows)
+    named = jnp.where(ids_ref[...] == me, gates_ref[...], 0)
+    high = jnp.sum(dot(repeat, lax.shift_right_logical(named, 8).astype(F32).astype(BF16)), axis=1, keepdims=True)
+    low = jnp.sum(dot(repeat, lax.bitwise_and(named, 255).astype(F32).astype(BF16)), axis=1, keepdims=True)
+    row_weight = (high * 256.0 + low) / 65536.0
+    span = GROUP * total
+    q_order = select(span, span, lambda o: div(rem(o, total), rows) * (GROUP * rows) + div(o, total) * rows + rem(o, rows))
+
+    arrive(send_q)
+    loads[0].wait()
+    loads[1].wait()
+
+    send_o = lambda k: remote(o_send.at[rem(me + k, n)], o_got.at[me], o_ss, o_rs, k)
+    send_s = lambda k: remote(s_send.at[rem(me + k, n)], s_got.at[me], s_ss, s_rs, k)
+
+    def attend(i, _):
+        g = rem(div(me, per_kv) + (kv - 1 - i), kv)
+        at = pl.ds(pl.multiple_of(g * HEAD_DIM, HEAD_DIM), HEAD_DIM)
+        block = q_all[:, pl.ds(pl.multiple_of(g * (GROUP * rows), GROUP * rows), GROUP * rows), :]
+        q = dot(q_order, block.reshape(span, HEAD_DIM)).astype(BF16)
+        s = dot(k_buf[:, at], q, 1, 1)
+        top = jnp.max(s, axis=0, keepdims=True)
+        p = jnp.exp2((s - top) * scale)
+        mass = jnp.sum(p, axis=0, keepdims=True)
+        o = dot(v_buf[:, at], p.astype(BF16), 0, 0)
+        lanes = own_heads * total
+        for j in range(per_kv):
+            t = g * per_kv + j
+            o_send[t] = o[:, j * lanes : (j + 1) * lanes].astype(BF16)
+            s_send[t, 0:1, :] = top[:, j * lanes : (j + 1) * lanes]
+            s_send[t, 1:2, :] = mass[:, j * lanes : (j + 1) * lanes]
+        for j in range(per_kv):
+            t = g * per_kv + j
+
+            @pl.when(t != me)
+            def _():
+                k = rem(t - me + n, n)
+                send_s(k).start()
+                send_o(k).start()
+
+        return 0
+
+    lax.fori_loop(0, kv, attend, 0)
+    o_got[me] = o_send[me]
+    s_got[me] = s_send[me]
+    arrive(send_s)
+    arrive(send_o)
+
+    tops, masses = s_got[:, 0:1, :], s_got[:, 1:2, :]
+    factor = jnp.exp2((tops - jnp.max(tops, axis=0, keepdims=True)) * scale)
+    mass = jnp.sum(masses * factor, axis=0)
+    out = o_got[0].astype(F32) * factor[0]
+    for d in range(1, n):
+        out = out + o_got[d].astype(F32) * factor[d]
+    attended = (out / mass).astype(BF16)
+
+    halves = [
+        dot(select(n * TILE, own_heads * total, lambda o, j=j: j * total + spread_rows(o)), attended, 1, 1)
+        for j in range(own_heads)
+    ]
+    lhs = jnp.concatenate(halves, axis=1)
+    loads[2].wait()
+    proj = None
+    for c in range(parts):
+        term = dot(jnp.where(part_of == c, lhs, 0.0).astype(BF16), wo_buf[:, c * cols : (c + 1) * cols])
+        proj = term if proj is None else proj + term
+    p_send[...] = proj.astype(BF16).reshape(n, TILE, cols)
+    send_p = lambda k: remote(p_send.at[rem(me + k, n)], p_got.at[me], p_ss, p_rs, k)
+    spread(send_p)
+    p_got[me] = p_send[me]
+    arrive(send_p)
+    stream = t_tmp[...]
+    for d in range(n):
+        stream = stream + p_got[d].astype(F32)
+    t_tmp[...] = stream
+    squares = jnp.broadcast_to(jnp.sum(stream * stream, axis=1, keepdims=True), (TILE, 128))
+    s_tmp[...] = squares
+    whole = s_tmp[0:rows, :]
+    for c in range(1, parts):
+        whole = whole + s_tmp[c * rows : (c + 1) * rows, :]
+    inverse = lax.rsqrt(whole[:, 0:1] / model + 1e-06)
+    for c in range(parts):
+        piece = t_tmp[c * rows : (c + 1) * rows, :]
+        hid_ref[:, c * cols : (c + 1) * cols] = piece.astype(BF16)
+        t_tmp[c * rows : (c + 1) * rows, :] = piece * inverse * gain_ref[:, c * cols : (c + 1) * cols]
+    n_all[me] = t_tmp[...].astype(BF16)
+    send_n = lambda k: remote(n_all.at[me], n_all.at[me], n_ss, n_rs, k)
+    spread(send_n)
+    by_part = select(n * TILE, n * TILE, lambda o: div(rem(o, total), rows) * TILE + div(o, total) * rows + rem(o, rows))
+    for load in loads[3:]:
+        load.wait()
+    arrive(send_n)
+
+    x = dot(by_part, n_all[...].reshape(n * TILE, cols)).astype(BF16)
+    gate = up = None
+    for c in range(parts):
+        piece = x[c * total : (c + 1) * total, :]
+        a, b = dot(piece, wg_buf[c * cols : (c + 1) * cols, :]), dot(piece, wu_buf[c * cols : (c + 1) * cols, :])
+        gate, up = (a, b) if gate is None else (gate + a, up + b)
+    inner = (gate / (1.0 + jnp.exp(-gate)) * up).astype(BF16)
+    lhs = dot(repeat, inner)
+    y = None
+    for c in range(parts):
+        term = dot(jnp.where(part_of == c, lhs, 0.0).astype(BF16), wd_buf[:, c * cols : (c + 1) * cols])
+        y = term if y is None else y + term
+    y_send[...] = (y * row_weight).astype(BF16).reshape(n, TILE, cols)
+    send_y = lambda k: remote(y_send.at[rem(me + k, n)], y_got.at[me], y_ss, y_rs, k)
+    spread(send_y)
+    y_got[me] = y_send[me]
+    for make in (send_q, send_s, send_o, send_p, send_n):
+        left(make)
+    arrive(send_y)
+    moe = y_got[0].astype(F32)
+    for d in range(1, n):
+        moe = moe + y_got[d].astype(F32)
+    t_tmp[...] = moe
+    for c in range(parts):
+        moe_ref[:, c * cols : (c + 1) * cols] = t_tmp[c * rows : (c + 1) * rows, :].astype(BF16)
+    left(send_y)
+
+
+def fused(n, queries, k_cache, v_cache, w_out, residual, gain, ids, gates, w_gate, w_up, w_down):
+    rows, width = queries.shape
+    model = residual.shape[1]
+    heads = width // HEAD_DIM
+    cols = model * rows // TILE
+    lanes = heads // n * n * rows
+    vmem, hbm = pl.BlockSpec(memory_space=pltpu.VMEM), pl.BlockSpec(memory_space=pl.ANY)
+    block = lambda *shape, kind=BF16: pltpu.VMEM(shape, kind)
+    message = block(n, TILE, cols)
+    return pl.pallas_call(
+        functools.partial(fused_kernel, n),
+        out_shape=(jax.ShapeDtypeStruct(residual.shape, BF16),) * 2,
+        in_specs=[vmem] * 5 + [hbm] * 6,
+        out_specs=(vmem, vmem),
+        scratch_shapes=[
+            block(*k_cache.shape), block(*v_cache.shape), block(*w_out.shape),
+            block(*w_gate.shape[1:]), block(*w_up.shape[1:]), block(*w_down.shape[1:]),
+            block(heads * rows, HEAD_DIM, kind=F32), block(TILE, cols, kind=F32), block(TILE, 128, kind=F32),
+            block(n, heads * rows, HEAD_DIM),
+            block(n, HEAD_DIM, lanes), block(n, HEAD_DIM, lanes),
+            block(n, 8, lanes, kind=F32), block(n, 8, lanes, kind=F32),
+            message, message, message, message, message,
+            pltpu.SemaphoreType.DMA((6,)),
+        ] + [pltpu.SemaphoreType.DMA((n,))] * 12,
+        compiler_params=pltpu.CompilerParams(
+            collective_id=0, has_side_effects=True, vmem_limit_bytes=48 * 2**20
+        ),
+    )(queries, residual, gain.reshape(1, model), ids, gates, k_cache, v_cache, w_out, w_gate, w_up, w_down)
+
+
 def solution(mesh):
+    n = mesh.shape["blk"]
+
+    def body(*blocks):
+        if fits_fused(n, *blocks):
+            return fused(n, *blocks)
+        return shards(*blocks)
+
     return jax.shard_map(
-        shards,
+        body,
         mesh=mesh,
         in_specs=(
             P(("groups", "blk"), None),

time: 311 us -> 69.5 us (0.22)
  waiting for transfers between devices: 112 us -> 0 us
  blocking collectives: 111 us -> 0 us
  Pallas kernels: 0 us -> 59.8 us
  matrix products: 20.6 us -> 0 us
  starting transfers between devices: 19.9 us -> 0 us
  local copies, waits for them, and re-layouts: 23.1 us -> 8.6 us
  between operations: 14.9 us -> 0.65 us
  other arithmetic: 7.85 us -> 0 us
    unnamed x2 -> x0, waiting for transfers between devices: 85.8 us -> none
    unnamed x1 -> x0, blocking collectives: 63.7 us -> none
    pallas_call x0 -> x1, Pallas kernels: none -> 59.8 us  [fused(): pl.pallas_call(functools.partial(fused_kernel, n), out_shape=(jax.ShapeDt...]
    all_gather x2 -> x0, blocking collectives: 47.8 us -> none  [the longest x1 26.3 us: shards(): every_query = lax.all_gather(queries, 'blk', axis=0, tiled=True)]
    all_to_all x4 -> x0, waiting for transfers between devices: 26.6 us -> none  [the longest x1 16.9 us: shards(): lax.all_to_all(part_out, 'blk', split_axis=0, concat_axis=0, tiled=True)]
    dot_general x8 -> x0, matrix products: 20.6 us -> none  [the longest x1 4.78 us: local_attend(): jnp.einsum('rhgc,chd->rhgd', probs.astype(jnp.bfloat16), value_three, pre...]
    all_to_all x4 -> x0, starting transfers between devices: 19.8 us -> none  [the longest x1 6.86 us: shards(): lax.all_to_all(attended, 'blk', split_axis=1, concat_axis=0, tiled=True)]
    reshape x3 -> x0, local copies, waits for them, and re-layouts: 6.95 us -> none  [the longest x1 2.4 us: local_attend(): query_four = query_rows.reshape(row_count, KV_HEADS, GROUP, HEAD_DIM)]
  transfers between devices with their start and end apart: 5 -> 0, of which waited for: 4 -> 0; matrix products, arithmetic and copies ran while one was open for 5% -> 0% of each run, Pallas kernels for 0% -> 0%
where the time goes in v1:
time: 69.5 us; the launch traced here: 69.1 us
  Pallas kernels  59.8 us (86%)
  local copies, waits for them, and re-layouts  8.6 us (12%)
    pallas_call x1, Pallas kernels, fused(): pl.pallas_call(functools.partial(fused_kernel, n), out_shape=(jax.ShapeDt...  59.8 us
    unnamed x16, local copies, waits for them, and re-layouts  8.6 us

profile of v1, /device:TPU:0, one launch (start us, length us, event | category | flops | bytes accessed | tf_op | source)
XLA Modules:
  0.0 69.1 jit_solution(8541610801685778756)
XLA Ops:
  0.6 0.8 %copy.13.ids_ref = s32[64,8]{1,0:T(8,128)S(1)} copy(s32[64,8]{0,1:T(8,128)} %param.17) | data formatting | bytes 4096 | tf_op args[6]
  1.4 0.8 %copy.14.gates_ref = s32[64,8]{1,0:T(8,128)S(1)} copy(s32[64,8]{0,1:T(8,128)} %param.18) | data formatting | bytes 4096 | tf_op args[7]
  2.2 0.0 copy-start
  2.2 1.2 %copy-done = bf16[1024,512]{1,0:T(8,128)(2,1)S(1)} copy-done((bf16[1024,512]{1,0:T(8,128)(2,1)S(1)}, bf16[1024,512]{1,0:T(8,128)(2,1)}, u32[]{:S(2)}) %copy-start) | copy-done | bytes 1048600
  3.4 0.0 copy-start.1
  3.4 1.2 %copy-done.1 = bf16[1024,512]{1,0:T(8,128)(2,1)S(1)} copy-done((bf16[1024,512]{1,0:T(8,128)(2,1)S(1)}, bf16[1024,512]{1,0:T(8,128)(2,1)}, u32[]{:S(2)}) %copy-start.1) | copy-done | bytes 1048600
  4.6 0.0 copy-start.2
  4.6 1.2 %copy-done.2 = bf16[256,2048]{1,0:T(8,128)(2,1)S(1)} copy-done((bf16[256,2048]{1,0:T(8,128)(2,1)S(1)}, bf16[256,2048]{1,0:T(8,128)(2,1)}, u32[]{:S(2)}) %copy-start.2) | copy-done | bytes 1048600
  5.8 0.0 copy-start.3
  5.8 0.8 %copy-done.3 = bf16[4,4096]{1,0:T(4,128)(2,1)S(1)} copy-done((bf16[4,4096]{1,0:T(4,128)(2,1)S(1)}, bf16[4,4096]{1,0:T(4,128)(2,1)}, u32[]{:S(2)}) %copy-start.3) | copy-done | bytes 32792
  6.6 0.0 copy-start.4
  6.6 0.7 %copy-done.4 = bf16[4,2048]{1,0:T(4,128)(2,1)S(1)} copy-done((bf16[4,2048]{1,0:T(4,128)(2,1)S(1)}, bf16[4,2048]{1,0:T(4,128)(2,1)}, u32[]{:S(2)}) %copy-start.4) | copy-done | bytes 16408
  7.3 0.0 copy-start.5
  7.3 0.7 %copy-done.5 = f32[2048]{0:T(1024)S(1)} copy-done((f32[2048]{0:T(1024)S(1)}, f32[2048]{0:T(1024)}, u32[]{:S(2)}) %copy-start.5) | copy-done | bytes 8216
  8.0 59.8 %shard_map.122 = (bf16[4,2048]{1,0:T(4,128)(2,1)S(1)}, bf16[4,2048]{1,0:T(4,128)(2,1)S(1)}) custom-call(bf16[4,4096]{1,0:T(4,128)(2,1)S(1)} %copy-done.3, bf16[4,2048]{1,0:T(4,128)(2,1)S(1)} %copy-done.4, f32[1,2048]{1,0:T(1,128)S(1)} %bitcast.1, s32[64,8]{1,0:T(8,128)S(1)} %copy.13.ids_ref, s32[64,8]{1,0:T(8,128)S(1)} %copy.14.gates_ref, ...), custom_call_target="tpu_custom_call" | custom-call | tf_op jit(solution)/shard_map/pallas_call | solution.py:363
  67.9 0.6 copy.17
  68.5 0.6 copy.18
Async XLA Ops:
  2.2 1.2 %copy-start = (bf16[1024,512]{1,0:T(8,128)(2,1)S(1)}, bf16[1024,512]{1,0:T(8,128)(2,1)}, u32[]{:S(2)}) copy-start(bf16[1024,512]{1,0:T(8,128)(2,1)} %k_hbm.1) | copy-start | bytes 3145732
  3.4 1.2 %copy-start.1 = (bf16[1024,512]{1,0:T(8,128)(2,1)S(1)}, bf16[1024,512]{1,0:T(8,128)(2,1)}, u32[]{:S(2)}) copy-start(bf16[1024,512]{1,0:T(8,128)(2,1)} %v_hbm.1) | copy-start | bytes 3145732
  4.6 1.2 %copy-start.2 = (bf16[256,2048]{1,0:T(8,128)(2,1)S(1)}, bf16[256,2048]{1,0:T(8,128)(2,1)}, u32[]{:S(2)}) copy-start(bf16[256,2048]{1,0:T(8,128)(2,1)} %wo_hbm.1) | copy-start | bytes 3145732
  5.8 0.8 %copy-start.3 = (bf16[4,4096]{1,0:T(4,128)(2,1)S(1)}, bf16[4,4096]{1,0:T(4,128)(2,1)}, u32[]{:S(2)}) copy-start(bf16[4,4096]{1,0:T(4,128)(2,1)} %q_ref.1) | copy-start | bytes 98308
  6.6 0.7 %copy-start.4 = (bf16[4,2048]{1,0:T(4,128)(2,1)S(1)}, bf16[4,2048]{1,0:T(4,128)(2,1)}, u32[]{:S(2)}) copy-start(bf16[4,2048]{1,0:T(4,128)(2,1)} %res_ref.1) | copy-start | bytes 49156
  7.3 0.7 %copy-start.5 = (f32[2048]{0:T(1024)S(1)}, f32[2048]{0:T(1024)}, u32[]{:S(2)}) copy-start(f32[2048]{0:T(1024)} %param.16) | copy-start | bytes 24580

commit v2 on v1

--- a/solution.py
+++ b/solution.py
@@ -134,7 +134,10 @@
     rows, width = queries.shape
     heads = width // HEAD_DIM
     return (
-        heads % n == 0
+        n % 4 == 0
+        and heads % n == 0
+        and (heads // GROUP) % 2 == 0
+        and (GROUP * n // heads) % 2 == 0
         and w_out.shape[0] % HEAD_DIM == 0
         and GROUP % (heads // n) == 0
         and (heads // n) * n * rows == HEAD_DIM
@@ -156,11 +159,13 @@
 
 
 def fused_kernel(
-    n, q_ref, res_ref, gain_ref, ids_ref, gates_ref, k_hbm, v_hbm, wo_hbm, wg_hbm, wu_hbm, wd_hbm,
+    n, q_hbm, res_hbm, gain_hbm, ids_hbm, gates_hbm, k_hbm, v_hbm, wo_hbm, wg_hbm, wu_hbm, wd_hbm,
     hid_ref, moe_ref,
+    q_ref, res_ref, gain_ref, ids_ref, gates_ref,
     k_buf, v_buf, wo_buf, wg_buf, wu_buf, wd_buf, q_tmp, t_tmp, s_tmp,
-    q_all, o_send, o_got, s_send, s_got, p_send, p_got, n_all, y_send, y_got,
+    q_send, q_all, q_perm, o_send, o_got, s_send, s_got, p_send, p_got, n_all, y_send, y_got,
     load_sem, q_ss, q_rs, o_ss, o_rs, s_ss, s_rs, p_ss, p_rs, n_ss, n_rs, y_ss, y_rs,
+    kv_ss, kv_rs, f_ss, f_rs,
 ):
     me = lax.axis_index("blk")
     rows, width = q_ref.shape
@@ -168,19 +173,24 @@
     heads = width // HEAD_DIM
     kv = heads // GROUP
     own_heads = heads // n
-    per_kv = GROUP // own_heads
+    half = n // 2
+    core, pair = lax.rem(me, 2), lax.div(me, 2)
+    mate = me + 1 - 2 * core
+    mine = heads // 2 * rows
     total = n * rows
     parts = TILE // rows
     cols = model // parts
     div, rem = lax.div, lax.rem
     scale = math.log2(math.e) / math.sqrt(HEAD_DIM)
 
-    loads = [
-        pltpu.make_async_copy(s, d, load_sem.at[i])
-        for i, (s, d) in enumerate(
-            ((k_hbm, k_buf), (v_hbm, v_buf), (wo_hbm, wo_buf), (wg_hbm.at[0], wg_buf), (wu_hbm.at[0], wu_buf), (wd_hbm.at[0], wd_buf))
-        )
-    ]
+    kv_cols = k_buf.shape[2]
+    kv_at = lambda which: pl.ds(pl.multiple_of(which * kv_cols, 128), kv_cols)
+    moves = (
+        (q_hbm, q_ref), (res_hbm, res_ref), (gain_hbm, gain_ref), (ids_hbm, ids_ref), (gates_hbm, gates_ref),
+        (k_hbm.at[:, kv_at(core)], k_buf.at[core]), (v_hbm.at[:, kv_at(core)], v_buf.at[core]),
+        (wo_hbm, wo_buf), (wg_hbm.at[0], wg_buf), (wu_hbm.at[0], wu_buf), (wd_hbm.at[0], wd_buf),
+    )
+    loads = [pltpu.make_async_copy(s, d, load_sem.at[i]) for i, (s, d) in enumerate(moves)]
     for load in loads:
         load.start()
 
@@ -219,12 +229,28 @@
 
         lax.fori_loop(1, n, step, 0)
 
+    def move(src, dst, ss, rs, peer):
+        return pltpu.make_async_remote_copy(
+            src_ref=src, dst_ref=dst, send_sem=ss, recv_sem=rs, device_id={"blk": peer}, device_id_type=MESH
+        )
+
+    loads[0].wait()
     for h in range(heads):
         q_tmp[h * rows : (h + 1) * rows, :] = q_ref[:, h * HEAD_DIM : (h + 1) * HEAD_DIM].astype(F32)
-    q_all[me] = q_tmp[...].astype(BF16)
+    for c in range(2):
+        q_send[c] = q_tmp[c * mine : (c + 1) * mine, :].astype(BF16)
+    q_all[me] = q_send[core]
     pl.semaphore_wait(barrier, n - 1)
-    send_q = lambda k: remote(q_all.at[me], q_all.at[me], q_ss, q_rs, k)
+    send_q = lambda k: remote(q_send.at[rem(rem(me + k, n), 2)], q_all.at[me], q_ss, q_rs, k)
     spread(send_q)
+    swaps = [
+        move(src.at[:, kv_at(1 - core)], dst.at[core], kv_ss.at[i], kv_rs.at[i], mate)
+        for i, (src, dst) in enumerate(((k_hbm, k_buf), (v_hbm, v_buf)))
+    ]
+    for swap in swaps:
+        swap.start()
+    for load in loads[1:5]:
+        load.wait()
 
     for c in range(parts):
         t_tmp[c * rows : (c + 1) * rows, :] = res_ref[:, c * cols : (c + 1) * cols].astype(F32)
@@ -232,57 +258,83 @@
     repeat = select(n * TILE, total, spread_rows)
     part_of = div(rem(lax.broadcasted_iota(jnp.int32, (n * TILE, 1), 0), TILE), rows)
     named = jnp.where(ids_ref[...] == me, gates_ref[...], 0)
-    high = jnp.sum(dot(repeat, lax.shift_right_logical(named, 8).astype(F32).astype(BF16)), axis=1, keepdims=True)
-    low = jnp.sum(dot(repeat, lax.bitwise_and(named, 255).astype(F32).astype(BF16)), axis=1, keepdims=True)
+    high = jnp.sum(dot(repeat, lax.shift_right_logical(named, 8).astype(F32).astype(BF16), 1, 1), axis=1, keepdims=True)
+    low = jnp.sum(dot(repeat, lax.bitwise_and(named, 255).astype(F32).astype(BF16), 1, 1), axis=1, keepdims=True)
     row_weight = (high * 256.0 + low) / 65536.0
     span = GROUP * total
     q_order = select(span, span, lambda o: div(rem(o, total), rows) * (GROUP * rows) + div(o, total) * rows + rem(o, rows))
 
     arrive(send_q)
-    loads[0].wait()
-    loads[1].wait()
-
-    send_o = lambda k: remote(o_send.at[rem(me + k, n)], o_got.at[me], o_ss, o_rs, k)
-    send_s = lambda k: remote(s_send.at[rem(me + k, n)], s_got.at[me], s_ss, s_rs, k)
+    lanes = own_heads * total
+    for g in range(kv // 2):
+        block = q_all[:, g * GROUP * rows : (g + 1) * GROUP * rows, :].reshape(span, HEAD_DIM)
+        ordered = dot(q_order, block).astype(BF16)
+        for u in range(span // (2 * lanes)):
+            q_perm[g * (span // (2 * lanes)) + u] = ordered[u * 2 * lanes : (u + 1) * 2 * lanes]
+    for load in loads[5:7]:
+        load.wait()
+    for swap in swaps:
+        swap.wait_recv()
+
+    def send_o(t):
+        return move(o_send.at[t], o_got.at[pair], o_ss.at[t], o_rs.at[pair], core * half + t)
+
+    def send_s(t):
+        return move(s_send.at[t], s_got.at[pair], s_ss.at[t], s_rs.at[pair], core * half + t)
+
+    steps = half // 2
+    per_step = steps // (kv // 2)
 
     def attend(i, _):
-        g = rem(div(me, per_kv) + (kv - 1 - i), kv)
-        at = pl.ds(pl.multiple_of(g * HEAD_DIM, HEAD_DIM), HEAD_DIM)
-        block = q_all[:, pl.ds(pl.multiple_of(g * (GROUP * rows), GROUP * rows), GROUP * rows), :]
-        q = dot(q_order, block.reshape(span, HEAD_DIM)).astype(BF16)
-        s = dot(k_buf[:, at], q, 1, 1)
+        u = rem(div(pair, 2) + i, steps)
+        at = pl.ds(pl.multiple_of(div(u, per_step) * HEAD_DIM, HEAD_DIM), HEAD_DIM)
+        keys = k_buf[:, :, at].reshape(2 * k_buf.shape[1], HEAD_DIM)
+        values = v_buf[:, :, at].reshape(2 * v_buf.shape[1], HEAD_DIM)
+        s = dot(keys, q_perm[u], 1, 1)
         top = jnp.max(s, axis=0, keepdims=True)
         p = jnp.exp2((s - top) * scale)
         mass = jnp.sum(p, axis=0, keepdims=True)
-        o = dot(v_buf[:, at], p.astype(BF16), 0, 0)
-        lanes = own_heads * total
-        for j in range(per_kv):
-            t = g * per_kv + j
+        o = dot(values, p.astype(BF16), 0, 0)
+        for j in range(2):
+            t = 2 * u + j
             o_send[t] = o[:, j * lanes : (j + 1) * lanes].astype(BF16)
             s_send[t, 0:1, :] = top[:, j * lanes : (j + 1) * lanes]
             s_send[t, 1:2, :] = mass[:, j * lanes : (j + 1) * lanes]
-        for j in range(per_kv):
-            t = g * per_kv + j
-
-            @pl.when(t != me)
+        for j in range(2):
+            t = 2 * u + j
+
+            @pl.when(core * half + t != me)
             def _():
-                k = rem(t - me + n, n)
-                send_s(k).start()
-                send_o(k).start()
+                send_s(t).start()
+                send_o(t).start()
 
         return 0
 
-    lax.fori_loop(0, kv, attend, 0)
-    o_got[me] = o_send[me]
-    s_got[me] = s_send[me]
-    arrive(send_s)
-    arrive(send_o)
+    lax.fori_loop(0, steps, attend, 0)
+    source_core = div(me, half)
+
+    @pl.when(source_core == core)
+    def _():
+        o_got[pair] = o_send[me - core * half]
+        s_got[pair] = s_send[me - core * half]
+
+    def got(s, _):
+        source = 2 * s + source_core
+
+        @pl.when(source != me)
+        def _():
+            move(s_send.at[0], s_got.at[s], s_ss.at[0], s_rs.at[s], source).wait_recv()
+            move(o_send.at[0], o_got.at[s], o_ss.at[0], o_rs.at[s], source).wait_recv()
+
+        return 0
+
+    lax.fori_loop(0, half, got, 0)
 
     tops, masses = s_got[:, 0:1, :], s_got[:, 1:2, :]
     factor = jnp.exp2((tops - jnp.max(tops, axis=0, keepdims=True)) * scale)
     mass = jnp.sum(masses * factor, axis=0)
     out = o_got[0].astype(F32) * factor[0]
-    for d in range(1, n):
+    for d in range(1, half):
         out = out + o_got[d].astype(F32) * factor[d]
     attended = (out / mass).astype(BF16)
 
@@ -291,7 +343,7 @@
         for j in range(own_heads)
     ]
     lhs = jnp.concatenate(halves, axis=1)
-    loads[2].wait()
+    loads[7].wait()
     proj = None
     for c in range(parts):
         term = dot(jnp.where(part_of == c, lhs, 0.0).astype(BF16), wo_buf[:, c * cols : (c + 1) * cols])
@@ -316,12 +368,40 @@
         hid_ref[:, c * cols : (c + 1) * cols] = piece.astype(BF16)
         t_tmp[c * rows : (c + 1) * rows, :] = piece * inverse * gain_ref[:, c * cols : (c + 1) * cols]
     n_all[me] = t_tmp[...].astype(BF16)
-    send_n = lambda k: remote(n_all.at[me], n_all.at[me], n_ss, n_rs, k)
-    spread(send_n)
+    def send_n(k):
+        return move(n_all.at[me], n_all.at[me], n_ss.at[k], n_rs.at[k], rem(me + 2 * k, n))
+
+    def got_n(k):
+        block = n_all.at[rem(me - 2 * k + n, n)]
+        return move(block, block, n_ss.at[k], n_rs.at[k], rem(me - 2 * k + n, n))
+
+    def hand_on(k):
+        block = n_all.at[rem(me - 2 * k + n, n)]
+        return move(block, block, f_ss.at[k], f_rs.at[k], mate)
+
+    def handed(k):
+        block = n_all.at[rem(mate - 2 * k + n, n)]
+        return move(block, block, f_ss.at[k], f_rs.at[k], mate)
+
+    def each(first, make):
+        def step(k, _):
+            make(k)
+            return 0
+
+        lax.fori_loop(first, half, step, 0)
+
+    each(1, lambda k: send_n(k).start())
+    hand_on(0).start()
     by_part = select(n * TILE, n * TILE, lambda o: div(rem(o, total), rows) * TILE + div(o, total) * rows + rem(o, rows))
-    for load in loads[3:]:
+    for load in loads[8:]:
         load.wait()
-    arrive(send_n)
+
+    def relay(k):
+        got_n(k).wait_recv()
+        hand_on(k).start()
+
+    each(1, relay)
+    each(0, lambda k: handed(k).wait_recv())
 
     x = dot(by_part, n_all[...].reshape(n * TILE, cols)).astype(BF16)
     gate = up = None
@@ -339,8 +419,20 @@
     send_y = lambda k: remote(y_send.at[rem(me + k, n)], y_got.at[me], y_ss, y_rs, k)
     spread(send_y)
     y_got[me] = y_send[me]
-    for make in (send_q, send_s, send_o, send_p, send_n):
-        left(make)
+    left(send_q)
+    for swap in swaps:
+        swap.wait_send()
+
+    def gone(t):
+        @pl.when(core * half + t != me)
+        def _():
+            send_s(t).wait_send()
+            send_o(t).wait_send()
+
+    each(0, gone)
+    left(send_p)
+    each(1, lambda k: send_n(k).wait_send())
+    each(0, lambda k: hand_on(k).wait_send())
     arrive(send_y)
     moe = y_got[0].astype(F32)
     for d in range(1, n):
@@ -363,22 +455,27 @@
     return pl.pallas_call(
         functools.partial(fused_kernel, n),
         out_shape=(jax.ShapeDtypeStruct(residual.shape, BF16),) * 2,
-        in_specs=[vmem] * 5 + [hbm] * 6,
+        in_specs=[hbm] * 11,
         out_specs=(vmem, vmem),
         scratch_shapes=[
-            block(*k_cache.shape), block(*v_cache.shape), block(*w_out.shape),
+            block(rows, width), block(rows, model), block(1, model, kind=F32),
+            block(*ids.shape[::-1], kind=jnp.int32), block(*gates.shape[::-1], kind=jnp.int32),
+            block(2, k_cache.shape[0], k_cache.shape[1] // 2), block(2, v_cache.shape[0], v_cache.shape[1] // 2),
+            block(*w_out.shape),
             block(*w_gate.shape[1:]), block(*w_up.shape[1:]), block(*w_down.shape[1:]),
             block(heads * rows, HEAD_DIM, kind=F32), block(TILE, cols, kind=F32), block(TILE, 128, kind=F32),
-            block(n, heads * rows, HEAD_DIM),
-            block(n, HEAD_DIM, lanes), block(n, HEAD_DIM, lanes),
-            block(n, 8, lanes, kind=F32), block(n, 8, lanes, kind=F32),
+            block(2, heads // 2 * rows, HEAD_DIM), block(n, heads // 2 * rows, HEAD_DIM),
+            block(n // 4, 2 * lanes, HEAD_DIM),
+            block(n // 2, HEAD_DIM, lanes), block(n // 2, HEAD_DIM, lanes),
+            block(n // 2, 8, lanes, kind=F32), block(n // 2, 8, lanes, kind=F32),
             message, message, message, message, message,
-            pltpu.SemaphoreType.DMA((6,)),
-        ] + [pltpu.SemaphoreType.DMA((n,))] * 12,
+            pltpu.SemaphoreType.DMA((11,)),
+        ] + [pltpu.SemaphoreType.DMA((n,))] * 12 + [pltpu.SemaphoreType.DMA((2,))] * 2
+        + [pltpu.SemaphoreType.DMA((n // 2,))] * 2,
         compiler_params=pltpu.CompilerParams(
-            collective_id=0, has_side_effects=True, vmem_limit_bytes=48 * 2**20
+            collective_id=0, has_side_effects=True, vmem_limit_bytes=60 * 2**20
         ),
-    )(queries, residual, gain.reshape(1, model), ids, gates, k_cache, v_cache, w_out, w_gate, w_up, w_down)
+    )(queries, residual, gain.reshape(1, model), ids.T, gates.T, k_cache, v_cache, w_out, w_gate, w_up, w_down)
 
 
 def solution(mesh):

time: 69.5 us -> 52.5 us (0.76)
  Pallas kernels: 59.8 us -> 48.9 us
  local copies, waits for them, and re-layouts: 8.6 us -> 2.66 us
    pallas_call x1, Pallas kernels: 59.8 us -> 48.9 us  [fused(): pl.pallas_call(functools.partial(fused_kernel, n), out_shape=(jax.ShapeDt...]
    unnamed x16 -> x2, local copies, waits for them, and re-layouts: 8.6 us -> 2.66 us
where the time goes in v2:
time: 52.5 us; the launch traced here: 52.2 us
  Pallas kernels  48.9 us (93%)
  local copies, waits for them, and re-layouts  2.66 us (5%)
  between operations  0.64 us (1%)
    pallas_call x1, Pallas kernels, fused(): pl.pallas_call(functools.partial(fused_kernel, n), out_shape=(jax.ShapeDt...  48.9 us
    unnamed x2, local copies, waits for them, and re-layouts  2.66 us

profile of v2, /device:TPU:0, one launch (start us, length us, event | category | flops | bytes accessed | tf_op | source)
XLA Modules:
  0.0 52.2 jit_solution(1837872668920964229)
XLA Ops:
  0.6 48.9 %shard_map.122 = (bf16[4,2048]{1,0:T(4,128)(2,1)}, bf16[4,2048]{1,0:T(4,128)(2,1)}) custom-call(bf16[4,4096]{1,0:T(4,128)(2,1)} %q_hbm.1, bf16[4,2048]{1,0:T(4,128)(2,1)} %res_hbm.1, f32[1,2048]{1,0:T(1,128)} %bitcast.3, s32[8,64]{1,0:T(8,128)} %bitcast.4, s32[8,64]{1,0:T(8,128)} %bitcast.5, bf16[1024,512]{1,0:T(8,128)(2,1)} %k_hbm.1, ...), custom_call_target="tpu_custom_call" | custom-call | tf_op jit(solution)/shard_map/pallas_call | solution.py:455
  49.5 1.3 %copy.15 = bf16[4,2048]{1,0:T(4,128)(2,1)} copy(bf16[4,2048]{1,0:T(4,128)(2,1)} %get-tuple-element.4) | data formatting | bytes 32768
  50.8 1.3 %copy.16 = bf16[4,2048]{1,0:T(4,128)(2,1)} copy(bf16[4,2048]{1,0:T(4,128)(2,1)} %get-tuple-element.5) | data formatting | bytes 32768

commit v3 on v2

--- a/solution.py
+++ b/solution.py
@@ -163,7 +163,7 @@
     hid_ref, moe_ref,
     q_ref, res_ref, gain_ref, ids_ref, gates_ref,
     k_buf, v_buf, wo_buf, wg_buf, wu_buf, wd_buf, q_tmp, t_tmp, s_tmp,
-    q_send, q_all, q_perm, o_send, o_got, s_send, s_got, p_send, p_got, n_all, y_send, y_got,
+    q_send, q_all, q_perm, f_loc, o_send, o_got, s_send, s_got, p_send, p_met, p_sum, p_got, n_all, y_send, y_met, y_sum, y_got,
     load_sem, q_ss, q_rs, o_ss, o_rs, s_ss, s_rs, p_ss, p_rs, n_ss, n_rs, y_ss, y_rs,
     kv_ss, kv_rs, f_ss, f_rs,
 ):
@@ -254,7 +254,8 @@
 
     for c in range(parts):
         t_tmp[c * rows : (c + 1) * rows, :] = res_ref[:, c * cols : (c + 1) * cols].astype(F32)
-    spread_rows = lambda o: div(o, TILE) * rows + rem(o, rows)
+    owner = lambda o: 2 * rem(div(o, TILE), half) + div(o, TILE * half)
+    spread_rows = lambda o: owner(o) * rows + rem(o, rows)
     repeat = select(n * TILE, total, spread_rows)
     part_of = div(rem(lax.broadcasted_iota(jnp.int32, (n * TILE, 1), 0), TILE), rows)
     named = jnp.where(ids_ref[...] == me, gates_ref[...], 0)
@@ -338,6 +339,25 @@
         out = out + o_got[d].astype(F32) * factor[d]
     attended = (out / mass).astype(BF16)
 
+    def across(ss, rs, out, met, sums, got):
+        swap = move(out, met, ss.at[0], rs.at[0], mate)
+
+        def ship(k):
+            to = rem(pair + k, half)
+            return move(sums.at[to], got.at[pair], ss.at[k], rs.at[k], 2 * to + core)
+
+        return swap, ship
+
+    def add_up(values, out, met, sums, got, swap, ship):
+        f_loc[...] = values.reshape(n, TILE, cols)
+        out[...] = f_loc[pl.ds((1 - core) * half, half)].astype(BF16)
+        swap.start()
+        swap.wait_recv()
+        sums[...] = (f_loc[pl.ds(core * half, half)] + met[...].astype(F32)).astype(BF16)
+        for k in range(1, half):
+            ship(k).start()
+        got[pair] = sums[pair]
+
     halves = [
         dot(select(n * TILE, own_heads * total, lambda o, j=j: j * total + spread_rows(o)), attended, 1, 1)
         for j in range(own_heads)
@@ -348,13 +368,13 @@
     for c in range(parts):
         term = dot(jnp.where(part_of == c, lhs, 0.0).astype(BF16), wo_buf[:, c * cols : (c + 1) * cols])
         proj = term if proj is None else proj + term
-    p_send[...] = proj.astype(BF16).reshape(n, TILE, cols)
-    send_p = lambda k: remote(p_send.at[rem(me + k, n)], p_got.at[me], p_ss, p_rs, k)
-    spread(send_p)
-    p_got[me] = p_send[me]
-    arrive(send_p)
+    swap_p, ship_p = across(p_ss, p_rs, p_send, p_met, p_sum, p_got)
+    add_up(proj, p_send, p_met, p_sum, p_got, swap_p, ship_p)
+    for k in range(1, half):
+        back = rem(pair - k + half, half)
+        move(p_sum.at[0], p_got.at[back], p_ss.at[k], p_rs.at[k], 2 * back + core).wait_recv()
     stream = t_tmp[...]
-    for d in range(n):
+    for d in range(half):
         stream = stream + p_got[d].astype(F32)
     t_tmp[...] = stream
     squares = jnp.broadcast_to(jnp.sum(stream * stream, axis=1, keepdims=True), (TILE, 128))
@@ -415,10 +435,8 @@
     for c in range(parts):
         term = dot(jnp.where(part_of == c, lhs, 0.0).astype(BF16), wd_buf[:, c * cols : (c + 1) * cols])
         y = term if y is None else y + term
-    y_send[...] = (y * row_weight).astype(BF16).reshape(n, TILE, cols)
-    send_y = lambda k: remote(y_send.at[rem(me + k, n)], y_got.at[me], y_ss, y_rs, k)
-    spread(send_y)
-    y_got[me] = y_send[me]
+    swap_y, ship_y = across(y_ss, y_rs, y_send, y_met, y_sum, y_got)
+    add_up(y * row_weight, y_send, y_met, y_sum, y_got, swap_y, ship_y)
     left(send_q)
     for swap in swaps:
         swap.wait_send()
@@ -430,17 +448,21 @@
             send_o(t).wait_send()
 
     each(0, gone)
-    left(send_p)
+    swap_p.wait_send()
+    each(1, lambda k: ship_p(k).wait_send())
     each(1, lambda k: send_n(k).wait_send())
     each(0, lambda k: hand_on(k).wait_send())
-    arrive(send_y)
+    for k in range(1, half):
+        back = rem(pair - k + half, half)
+        move(y_sum.at[0], y_got.at[back], y_ss.at[k], y_rs.at[k], 2 * back + core).wait_recv()
     moe = y_got[0].astype(F32)
-    for d in range(1, n):
+    for d in range(1, half):
         moe = moe + y_got[d].astype(F32)
     t_tmp[...] = moe
     for c in range(parts):
         moe_ref[:, c * cols : (c + 1) * cols] = t_tmp[c * rows : (c + 1) * rows, :].astype(BF16)
-    left(send_y)
+    swap_y.wait_send()
+    each(1, lambda k: ship_y(k).wait_send())
 
 
 def fused(n, queries, k_cache, v_cache, w_out, residual, gain, ids, gates, w_gate, w_up, w_down):
@@ -451,7 +473,7 @@
     lanes = heads // n * n * rows
     vmem, hbm = pl.BlockSpec(memory_space=pltpu.VMEM), pl.BlockSpec(memory_space=pl.ANY)
     block = lambda *shape, kind=BF16: pltpu.VMEM(shape, kind)
-    message = block(n, TILE, cols)
+    part = block(n // 2, TILE, cols)
     return pl.pallas_call(
         functools.partial(fused_kernel, n),
         out_shape=(jax.ShapeDtypeStruct(residual.shape, BF16),) * 2,
@@ -465,10 +487,10 @@
             block(*w_gate.shape[1:]), block(*w_up.shape[1:]), block(*w_down.shape[1:]),
             block(heads * rows, HEAD_DIM, kind=F32), block(TILE, cols, kind=F32), block(TILE, 128, kind=F32),
             block(2, heads // 2 * rows, HEAD_DIM), block(n, heads // 2 * rows, HEAD_DIM),
-            block(n // 4, 2 * lanes, HEAD_DIM),
+            block(n // 4, 2 * lanes, HEAD_DIM), block(n, TILE, cols, kind=F32),
             block(n // 2, HEAD_DIM, lanes), block(n // 2, HEAD_DIM, lanes),
             block(n // 2, 8, lanes, kind=F32), block(n // 2, 8, lanes, kind=F32),
-            message, message, message, message, message,
+            *(part,) * 4, block(n, TILE, cols), *(part,) * 4,
             pltpu.SemaphoreType.DMA((11,)),
         ] + [pltpu.SemaphoreType.DMA((n,))] * 12 + [pltpu.SemaphoreType.DMA((2,))] * 2
         + [pltpu.SemaphoreType.DMA((n // 2,))] * 2,

time: 52.5 us -> 50.2 us (0.956)
  Pallas kernels: 48.9 us -> 46.5 us
    pallas_call x1, Pallas kernels: 48.9 us -> 46.5 us  [fused(): pl.pallas_call(functools.partial(fused_kernel, n), out_shape=(jax.ShapeDt...]
where the time goes in v3:
time: 50.2 us; the launch traced here: 49.8 us
  Pallas kernels  46.5 us (93%)
  local copies, waits for them, and re-layouts  2.66 us (5%)
  between operations  0.64 us (1%)
    pallas_call x1, Pallas kernels, fused(): pl.pallas_call(functools.partial(fused_kernel, n), out_shape=(jax.ShapeDt...  46.5 us
    unnamed x2, local copies, waits for them, and re-layouts  2.66 us

profile of v3, /device:TPU:0, one launch (start us, length us, event | category | flops | bytes accessed | tf_op | source)
XLA Modules:
  0.0 49.8 jit_solution(6129790200803386613)
XLA Ops:
  0.6 46.5 %shard_map.122 = (bf16[4,2048]{1,0:T(4,128)(2,1)}, bf16[4,2048]{1,0:T(4,128)(2,1)}) custom-call(bf16[4,4096]{1,0:T(4,128)(2,1)} %q_hbm.1, bf16[4,2048]{1,0:T(4,128)(2,1)} %res_hbm.1, f32[1,2048]{1,0:T(1,128)} %bitcast.3, s32[8,64]{1,0:T(8,128)} %bitcast.4, s32[8,64]{1,0:T(8,128)} %bitcast.5, bf16[1024,512]{1,0:T(8,128)(2,1)} %k_hbm.1, ...), custom_call_target="tpu_custom_call" | custom-call | tf_op jit(solution)/shard_map/pallas_call | solution.py:477
  47.2 1.3 %copy.15 = bf16[4,2048]{1,0:T(4,128)(2,1)} copy(bf16[4,2048]{1,0:T(4,128)(2,1)} %get-tuple-element.4) | data formatting | bytes 32768
  48.5 1.3 %copy.16 = bf16[4,2048]{1,0:T(4,128)(2,1)} copy(bf16[4,2048]{1,0:T(4,128)(2,1)} %get-tuple-element.5) | data formatting | bytes 32768
